TPU v7x, 1024 devices: a whole 8x8x8 slice. The times are simulated.
1024 devices in a mesh: dp: 64 (over x, z_hi, core), tensor: 16 (over y, z_lo).
Axes of the slice: x: 8, y: 8, z: 8 (z_hi: 4, z_lo: 2; z = z_hi * 2 + z_lo), core: 2. Of those that a mesh axis runs over, the one named last changes fastest.
Arguments:
- inputs: bfloat16 [16384, 4096], P('dp', 'tensor'), may hold values from -6 to 6
- first_factor: bfloat16 [256, 16, 1024], P(None, 'tensor'), may hold values from -0.375 to 0.375
- second_factor: bfloat16 [1024, 16, 1024], P(None, 'tensor'), may hold values from -0.1875 to 0.1875
- cotangent: bfloat16 [16384, 16384], P('tensor', 'dp'), may hold values from -6 to 6
Outputs:
- input_grad: bfloat16 [16384, 4096], P('dp', 'tensor')
- first_grad: float32 [256, 16, 1024], P('dp', 'tensor')
All inputs are finite; a program needn't handle non-finite values.
Results may differ from a plain program's by a relative error of at most 0.0063.
Values may be sent and summed in bfloat16 or wider, within the bound.
A program may use at most 32 MiB of HBM per device.

v0:
```python
import jax
import jax.numpy as jnp
from jax import lax
from jax.sharding import PartitionSpec as P


def gelu_backward(pre_act, upstream):
    value, pullback = jax.vjp(lambda v: jax.nn.gelu(v, approximate=True), pre_act)
    return pullback(upstream)[0]


def body(inputs, first_factor, second_factor, cotangent):
    tokens_here = inputs.shape[0]
    in_width = first_factor.shape[0]
    local = first_factor.shape[1]
    out_width = first_factor.shape[2]
    blocks = local * lax.axis_size("tensor")
    group = out_width // blocks
    block_grouped = inputs.reshape(tokens_here, local, in_width)
    split_first = first_factor.reshape(in_width, local, blocks, group)
    outgoing = jnp.einsum(
        "tlk,kljg->jlgt", block_grouped, split_first, preferred_element_type=jnp.float32
    ).astype(jnp.bfloat16)
    arrived = lax.all_to_all(outgoing, "tensor", split_axis=0, concat_axis=1, tiled=True)
    mixed = arrived.reshape(local, out_width, tokens_here)
    pre_act = jnp.einsum("lmt,mln->lnt", mixed, second_factor, preferred_element_type=jnp.float32)
    upstream = cotangent.reshape(local, out_width, tokens_here).astype(jnp.float32)
    pre_grad = gelu_backward(pre_act, upstream).astype(jnp.bfloat16)
    mixed_grad = jnp.einsum(
        "lnt,mln->lmt", pre_grad, second_factor, preferred_element_type=jnp.float32
    ).astype(jnp.bfloat16)
    returned = lax.all_to_all(
        mixed_grad.reshape(local, blocks, group, tokens_here),
        "tensor",
        split_axis=1,
        concat_axis=0,
        tiled=True,
    )
    input_grad = jnp.einsum(
        "jlgt,kljg->tlk", returned, split_first, preferred_element_type=jnp.float32
    )
    input_grad = input_grad.reshape(tokens_here, local * in_width).astype(jnp.bfloat16)
    factor = (tokens_here * lax.axis_size("dp")) ** (-0.5)
    first_term = jnp.einsum(
        "tlk,jlgt->kljg", block_grouped, returned, preferred_element_type=jnp.float32
    ).reshape(in_width, local, out_width)
    first_sum = lax.psum_scatter(first_term, "dp", scatter_dimension=0, tiled=True)
    return (input_grad, first_sum * factor)


def solution(mesh):
    return jax.shard_map(
        body,
        mesh=mesh,
        in_specs=(
            P("dp", "tensor"),
            P(None, "tensor", None),
            P(None, "tensor", None),
            P("tensor", "dp"),
        ),
        out_specs=(P("dp", "tensor"), P("dp", "tensor", None)),
        check_vma=False,
    )
```

profile of v0, /device:TPU:1, one launch (start us, length us, event | category | flops | bytes accessed | tf_op | source)
XLA Modules:
  0.0 646.3 jit_solution(11152127797996530830)
XLA Ops:
  7.2 0.0 copy-start
  7.2 0.0 copy-start.3
  7.2 1.4 copy.16
  8.6 0.0 copy-start.1
  8.6 2.2 fusion.13
  10.8 11.0 %all-to-all-start = ((bf16[16,1,64,256]{3,2,1,0:T(8,128)(2,1)}), bf16[16,1,64,256]{3,2,1,0:T(8,128)(2,1)}, u32[]{:S(2)}, u32[]{:S(2)}) async-start(bf16[16,1,64,256]{3,2,1,0:T(8,128)(2,1)} %fusion.13), calls=%async_computation | async-start | bytes 1048576 | tf_op jit(solution)/shard_map/all_to_all | solution.py:24
  21.8 0.0 all-reduce.3.cloned.1.call-start
  21.8 0.0 copy-done.3
  21.8 1.0 copy.15
  22.8 10.9 %all-to-all-done = bf16[16,1,64,256]{3,2,1,0:T(8,128)(2,1)} async-done(((bf16[16,1,64,256]{3,2,1,0:T(8,128)(2,1)}), bf16[16,1,64,256]{3,2,1,0:T(8,128)(2,1)}, u32[]{:S(2)}, u32[]{:S(2)}) %all-to-all-start) | async-done | bytes 524320 | tf_op jit(solution)/shard_map/all_to_all | solution.py:24
  33.7 0.0 copy-done
  33.7 4.0 fusion.10
  37.7 0.0 copy-done.1
  37.7 0.0 copy-start.4
  37.7 1.3 copy.18
  39.0 14.5 %all_to_all.8 = bf16[1,16,64,256]{3,2,0,1:T(8,128)(2,1)S(1)} all-to-all(bf16[1,16,64,256]{3,2,0,1:T(8,128)(2,1)S(1)} %bitcast.58), channel_id=1, replica_groups=mesh['dp'=64,'tensor'=16] {'tensor'}, dimensions={1} | all-to-all | bytes 1048576 | tf_op jit(solution)/shard_map/all_to_all | solution.py:32
  53.5 0.0 copy-start.2
  53.5 0.8 copy-done.2
  54.3 0.0 copy-done.4
  54.3 0.3 fusion.29
  54.6 1.9 copy.20
  56.5 0.0 all-reduce.3.cloned.1.call-update
  56.5 1.3 dynamic-slice
  58.5 2.2 fusion.14
  60.7 577.4 %all-reduce.3.cloned.1.call-done = f32[256,1,1024]{2,1,0:T(1,128)} async-done(((f32[256,1,1024]{2,1,0:T(1,128)}), f32[256,1,1024]{2,1,0:T(1,128)}) %all-reduce.3.cloned.1.call-update) | async-done | bytes 1048592
  638.1 1.3 dynamic-slice_multiply_fusion
Async XLA Ops:
  7.2 26.6 %copy-start = (bf16[1024,1,1024]{2,0,1:T(8,128)(2,1)S(1)}, bf16[1024,1,1024]{2,0,1:T(8,128)(2,1)}, u32[]{:S(2)}) copy-start(bf16[1024,1,1024]{2,0,1:T(8,128)(2,1)} %param.6) | copy-start | bytes 6291460
  7.2 14.7 %copy-start.3 = (bf16[1024,256]{1,0:T(8,128)(2,1)S(1)}, bf16[1024,256]{1,0:T(8,128)(2,1)}, u32[]{:S(2)}) copy-start(bf16[1024,256]{1,0:T(8,128)(2,1)} %param.7) | copy-start | bytes 1572868
  8.6 29.1 %copy-start.1 = (bf16[256,1,1024]{0,2,1:T(8,128)(2,1)}, bf16[256,1,1024]{0,2,1:T(8,128)(2,1)S(1)}, u32[]{:S(2)}) copy-start(bf16[256,1,1024]{0,2,1:T(8,128)(2,1)S(1)} %copy.16) | copy-start | bytes 1572868
  10.8 22.9 %all-to-all-start = ((bf16[16,1,64,256]{3,2,1,0:T(8,128)(2,1)}), bf16[16,1,64,256]{3,2,1,0:T(8,128)(2,1)}, u32[]{:S(2)}, u32[]{:S(2)}) async-start(bf16[16,1,64,256]{3,2,1,0:T(8,128)(2,1)} %fusion.13), calls=%async_computation | async-start | bytes 1048576 | tf_op jit(solution)/shard_map/all_to_all | solution.py:24
  21.8 616.3 %all-reduce.3.cloned.1.call-start = ((), (), s32[]{:S(2)}) async-start(), calls=%async_computation.2 | async-start | bytes 2097152
  37.7 16.6 %copy-start.4 = (bf16[256,256]{1,0:T(8,128)(2,1)S(1)}, bf16[256,256]{1,0:T(8,128)(2,1)}, u32[]{:S(2)}) copy-start(bf16[256,256]{1,0:T(8,128)(2,1)} %param.4) | copy-start | bytes 393220
  53.5 0.8 copy-start.2
Sparse Core Ops, SparseCore 0:
  56.7 581.4 all-reduce.2
where the time goes:
time: 647 us; the launch traced here: 646 us
  waiting for transfers between devices  588 us (91%)
  between operations  14.7 us (2%)
  blocking collectives  14.5 us (2%)
  starting transfers between devices  11 us (2%)
  matrix products  8.65 us (1%)
  local copies, waits for them, and re-layouts  7.72 us (1%)
    unnamed x2, waiting for transfers between devices  577 us
    all_to_all x1, blocking collectives, body(): lax.all_to_all(mixed_grad.reshape(local, blocks, group, tokens_here), 'te...  14.5 us
  transfers between devices with their start and end apart: 2, of which 2 were waited for; matrix products, arithmetic and copies ran while one was open for 1% of the time, Pallas kernels for 0%

commit v1 on v0

v1 whole, which is shorter than its diff:
```python
import functools

import jax
import jax.numpy as jnp
from jax import lax
from jax.experimental import pallas as pl
from jax.experimental.pallas import tpu as pltpu
from jax.sharding import PartitionSpec as P

MESH = pl.DeviceIdType.MESH
BF16, F32 = jnp.bfloat16, jnp.float32

Z_HI, CORES, Z_LO = 4, 2, 2


def gelu_slope(v):
    root = 0.7978845608028654
    square = v * v
    t = jnp.tanh(root * (v + 0.044715 * (square * v)))
    return 0.5 * (1.0 + t) + (0.5 * v) * (1.0 - t * t) * (root * (1.0 + 3.0 * 0.044715 * square))


def dot(a, b, contract=((1,), (0,))):
    return lax.dot_general(a, b, (contract, ((), ())), preferred_element_type=F32)


def kernel(
    dims, scale,
    x_hbm, f_hbm, s_hbm, cot_hbm,
    ig_ref, fg_ref,
    x_ref, f_ref, s_ref, cot_ref, st_ref, xpt_ref, pg_ref,
    out_buf, mix_buf, grad_buf, ret_buf,
    term_buf, core_land, x_send, x_land, z_send, z_land,
    load_sem, out_ssem, out_rsem, ret_ssem, ret_rsem,
    core_ssem, core_rsem, x_ssem, x_rsem, z_ssem, z_rsem,
):
    nx, nz, ny, chunks, groups = dims
    per = ny // groups
    nt = ny * Z_LO
    tokens, width = x_ref.shape
    hidden = f_ref.shape[1]
    span = hidden // nt
    pair = span * Z_LO
    tc = tokens // chunks
    rows = width // (nx * nz * CORES)

    dp, tp = lax.axis_index("dp"), lax.axis_index("tensor")
    x = dp // (nz * CORES)
    z = lax.rem(dp // CORES, nz)
    core = lax.rem(dp, CORES)
    y, zl = tp // Z_LO, lax.rem(tp, Z_LO)

    def dp_of(xi, zi, ci):
        return (xi * nz + zi) * CORES + ci

    def shift(s):
        return ny // 2 + (1 - 2 * lax.rem(s, 2)) * ((s + 1) // 2)

    def y_to(s):
        return lax.rem(y + shift(s), ny)

    def y_from(s):
        return lax.rem(y + ny - shift(s), ny)

    loads = [
        pltpu.make_async_copy(src, dst, load_sem.at[i])
        for i, (src, dst) in enumerate(
            ((x_hbm, x_ref), (f_hbm, f_ref), (s_hbm, s_ref), (cot_hbm, cot_ref))
        )
    ]
    for load in loads:
        load.start()

    barrier = pltpu.get_barrier_semaphore()

    def greet(i, _):
        to = lax.rem(tp + i, nt)
        pl.semaphore_signal(barrier, inc=1, device_id=(dp, to), device_id_type=MESH)
        return 0

    lax.fori_loop(1, nt, greet, 0)

    def greet_x(i, _):
        to = dp_of(lax.rem(x + i, nx), z, core)
        pl.semaphore_signal(barrier, inc=1, device_id=(to, tp), device_id_type=MESH)
        return 0

    lax.fori_loop(1, nx, greet_x, 0)

    def greet_z(i, _):
        to = dp_of(x, lax.rem(z + i, nz), core)
        pl.semaphore_signal(barrier, inc=1, device_id=(to, tp), device_id_type=MESH)
        return 0

    lax.fori_loop(1, nz, greet_z, 0)
    sibling = dp_of(x, z, 1 - core)
    pl.semaphore_signal(barrier, inc=1, device_id=(sibling, tp), device_id_type=MESH)

    def exchange(src, dst, ssem, rsem, c, s, dz):
        to = y_to(s) * Z_LO + lax.rem(zl + dz, Z_LO)
        i = s * Z_LO + dz
        return pltpu.make_async_remote_copy(
            src.at[c, to], dst.at[c, tp], ssem.at[c, i], rsem.at[c, i],
            device_id=(dp, to), device_id_type=MESH,
        )

    def landed(dst, ssem, rsem, c, s, dz):
        here = y_from(s) * Z_LO + lax.rem(zl + dz, Z_LO)
        i = s * Z_LO + dz
        pltpu.make_async_remote_copy(
            dst.at[c, here], dst.at[c, here], ssem.at[c, i], rsem.at[c, i],
            device_id=(dp, tp), device_id_type=MESH,
        ).wait_recv()

    def send_out(c, s, dz):
        exchange(out_buf, mix_buf, out_ssem, out_rsem, c, s, dz).start()

    def send_ret(c, s, dz):
        exchange(grad_buf, ret_buf, ret_ssem, ret_rsem, c, s, dz).start()

    loads[0].wait()
    loads[1].wait()

    def first(s):
        to = y_to(s)
        block = f_ref[:, pl.ds(pl.multiple_of(to * pair, pair), pair)]
        made = dot(block, x_ref[...], ((0,), (1,))).astype(BF16)
        for c in range(chunks):
            out_buf[c, pl.ds(to * Z_LO, Z_LO)] = made[:, c * tc : (c + 1) * tc].reshape(Z_LO, span, tc)

    first(0)
    pl.semaphore_wait(barrier, (nt - 1) + (nx - 1) + (nz - 1) + 1)
    for dz in range(Z_LO):
        send_out(0, 0, dz)

    def first_step(s, _):
        first(s)
        for dz in range(Z_LO):
            send_out(0, s, dz)
        return 0

    lax.fori_loop(1, ny - 1, first_step, 0)
    first(ny - 1)
    send_out(0, ny - 1, 1)
    for c in range(chunks):
        mix_buf[c, tp] = out_buf[c, tp]
    for c in range(1, chunks):

        def rest(s, _):
            for dz in range(Z_LO):
                send_out(c, s, dz)
            return 0

        lax.fori_loop(0, ny - 1, rest, 0)
        send_out(c, ny - 1, 1)

    row = lax.broadcasted_iota(jnp.int32, (width, width), 0)
    col = lax.broadcasted_iota(jnp.int32, (width, width), 1)
    half = width // CORES
    r_in = row & (rows - 1)
    z_in = (row & (rows * nz - 1)) - r_in
    x_in = (row & (half - 1)) - z_in - r_in
    c_in = jnp.where(row >= half, rows, 0)
    pick = jnp.where(x_in * CORES + z_in * CORES + c_in + r_in == col, 1.0, 0.0).astype(BF16)
    xpt_ref[...] = dot(pick, x_ref[...], ((1,), (1,))).astype(BF16)
    loads[2].wait()
    tile = min(256, hidden)
    for i in range(hidden // tile):
        st_ref[:, i * tile : (i + 1) * tile] = s_ref[i * tile : (i + 1) * tile, :].T
    loads[3].wait()

    for c in range(chunks):

        def arrive(s, _):
            for dz in range(Z_LO):
                landed(mix_buf, out_ssem, out_rsem, c, s, dz)
            return 0

        lax.fori_loop(0, ny - 1, arrive, 0)
        landed(mix_buf, out_ssem, out_rsem, c, ny - 1, 1)

        def forward(i, _):
            at = pl.ds(pl.multiple_of(i * tile, tile), tile)
            mixed = mix_buf[c].reshape(hidden, tc)
            v = dot(st_ref[at, :], mixed)
            up = cot_ref[at, c * tc : (c + 1) * tc].astype(F32)
            pg_ref[at, :] = (up * gelu_slope(v)).astype(BF16)
            return 0

        lax.fori_loop(0, hidden // tile, forward, 0)

        def back(s):
            to = y_to(s)
            block = s_ref[pl.ds(pl.multiple_of(to * pair, pair), pair), :]
            made = dot(block, pg_ref[...]).astype(BF16)
            grad_buf[c, pl.ds(to * Z_LO, Z_LO)] = made.reshape(Z_LO, span, tc)

        def back_step(s, _):
            back(s)
            for dz in range(Z_LO):
                send_ret(c, s, dz)
            return 0

        lax.fori_loop(0, ny - 1, back_step, 0)
        back(ny - 1)
        send_ret(c, ny - 1, 1)
        ret_buf[c, tp] = grad_buf[c, tp]

    def to_core(g):
        return pltpu.make_async_remote_copy(
            term_buf.at[g, 1 - core], core_land.at[g], core_ssem.at[g], core_rsem.at[g],
            device_id=(sibling, tp), device_id_type=MESH,
        )

    def to_x(g, i):
        other = lax.rem(x + i, nx)
        return pltpu.make_async_remote_copy(
            x_send.at[g, other], x_land.at[g, i], x_ssem.at[g, i], x_rsem.at[g, i],
            device_id=(dp_of(other, z, core), tp), device_id_type=MESH,
        )

    def to_z(g, i):
        other = lax.rem(z + i, nz)
        return pltpu.make_async_remote_copy(
            z_send.at[g, other], z_land.at[g, i], z_ssem.at[g, i], z_rsem.at[g, i],
            device_id=(dp_of(x, other, core), tp), device_id_type=MESH,
        )

    def stage_a(g):
        for p in range(per):
            s = g * per + p
            for c in range(chunks):
                for dz in range(Z_LO):
                    if s < ny - 1 or dz:
                        landed(ret_buf, ret_ssem, ret_rsem, c, s, dz)
            at = pl.ds(y_from(s) * Z_LO, Z_LO)
            term = jnp.zeros((width, pair), F32)
            for c in range(chunks):
                term += dot(
                    xpt_ref[:, c * tc : (c + 1) * tc], ret_buf[c, at].reshape(pair, tc), ((1,), (1,))
                )
            term_buf[g, 0, p] = term[:half]
            term_buf[g, 1, p] = term[half:]
        to_core(g).start()

    def stage_b(g):
        to_core(g).wait_recv()
        for p in range(per):
            total = term_buf[g, core, p] + core_land[g, p]
            core_land[g, p] = total
            x_send[g, :, p] = total.astype(BF16).reshape(nx, half // nx, pair)

        def go(i, _):
            to_x(g, i).start()
            return 0

        lax.fori_loop(1, nx, go, 0)

    def stage_c(g):
        part = half // nx

        def arrive(i, _):
            to_x(g, i).wait_recv()
            return 0

        lax.fori_loop(1, nx, arrive, 0)
        total = core_land[g, :, pl.ds(pl.multiple_of(x * part, part), part)]
        for i in range(1, nx):
            total += x_land[g, i].astype(F32)
        for i in range(nz):
            z_send[g, i] = total[:, i * rows : (i + 1) * rows]

        def go(i, _):
            to_z(g, i).start()
            return 0

        lax.fori_loop(1, nz, go, 0)

    def stage_d(g):
        def arrive(i, _):
            to_z(g, i).wait_recv()
            return 0

        lax.fori_loop(1, nz, arrive, 0)
        total = z_send[g, z]
        for i in range(1, nz):
            total += z_land[g, i]
        for p in range(per):
            at = pl.ds(pl.multiple_of(y_from(g * per + p) * pair, pair), pair)
            fg_ref[:, at] = total[p] * scale

    def input_grad():
        for c in range(chunks):
            made = dot(f_ref[...], ret_buf[c].reshape(hidden, tc))
            ig_ref[c * tc : (c + 1) * tc, :] = made.T.astype(BF16)

    for i in range(groups + 3):
        if i < groups:
            stage_a(i)
        if i == groups - 1:
            input_grad()
        if 0 <= i - 1 < groups:
            stage_b(i - 1)
        if 0 <= i - 2 < groups:
            stage_c(i - 2)
        if 0 <= i - 3 < groups:
            stage_d(i - 3)

    for c in range(chunks):

        def gone(s, _):
            for dz in range(Z_LO):
                exchange(out_buf, mix_buf, out_ssem, out_rsem, c, s, dz).wait_send()
                exchange(grad_buf, ret_buf, ret_ssem, ret_rsem, c, s, dz).wait_send()
            return 0

        lax.fori_loop(0, ny - 1, gone, 0)
        exchange(out_buf, mix_buf, out_ssem, out_rsem, c, ny - 1, 1).wait_send()
        exchange(grad_buf, ret_buf, ret_ssem, ret_rsem, c, ny - 1, 1).wait_send()
    for g in range(groups):
        to_core(g).wait_send()

        def gone_x(i, _):
            to_x(g, i).wait_send()
            return 0

        lax.fori_loop(1, nx, gone_x, 0)

        def gone_z(i, _):
            to_z(g, i).wait_send()
            return 0

        lax.fori_loop(1, nz, gone_z, 0)


def body(n_dp, n_tensor, z_hi, inputs, first_factor, second_factor, cotangent):
    tokens, width = inputs.shape
    hidden = first_factor.shape[2]
    nz, ny = z_hi, n_tensor // Z_LO
    nx = n_dp // (nz * CORES)
    chunks, groups = 2, min(4, ny)
    per = ny // groups
    tc = tokens // chunks
    span = hidden // n_tensor
    pair = span * Z_LO
    half = width // CORES
    part = half // nx
    rows = part // nz
    dma = pltpu.SemaphoreType.DMA
    flow = pltpu.VMEM((chunks, n_tensor, span, tc), BF16)
    input_grad, first_grad = pl.pallas_call(
        functools.partial(kernel, (nx, nz, ny, chunks, groups), (tokens * n_dp) ** (-0.5)),
        out_shape=(
            jax.ShapeDtypeStruct((tokens, width), BF16),
            jax.ShapeDtypeStruct((rows, hidden), F32),
        ),
        in_specs=[pl.BlockSpec(memory_space=pl.ANY)] * 4,
        out_specs=[pl.BlockSpec(memory_space=pltpu.VMEM)] * 2,
        scratch_shapes=[
            pltpu.VMEM((tokens, width), BF16),
            pltpu.VMEM((width, hidden), BF16),
            pltpu.VMEM((hidden, hidden), BF16),
            pltpu.VMEM((hidden, tokens), BF16),
            pltpu.VMEM((hidden, hidden), BF16),
            pltpu.VMEM((width, tokens), BF16),
            pltpu.VMEM((hidden, tc), BF16),
            flow, flow, flow, flow,
            pltpu.VMEM((groups, CORES, per, half, pair), F32),
            pltpu.VMEM((groups, per, half, pair), F32),
            pltpu.VMEM((groups, nx, per, part, pair), BF16),
            pltpu.VMEM((groups, nx, per, part, pair), BF16),
            pltpu.VMEM((groups, nz, per, rows, pair), F32),
            pltpu.VMEM((groups, nz, per, rows, pair), F32),
            dma((4,)),
            dma((chunks, n_tensor)), dma((chunks, n_tensor)),
            dma((chunks, n_tensor)), dma((chunks, n_tensor)),
            dma((groups,)), dma((groups,)),
            dma((groups, nx)), dma((groups, nx)),
            dma((groups, nz)), dma((groups, nz)),
        ],
        compiler_params=pltpu.CompilerParams(
            collective_id=0, has_side_effects=True, vmem_limit_bytes=40 * 2**20
        ),
        cost_estimate=pl.CostEstimate(
            flops=2 * tokens * hidden * (2 * hidden + 3 * width),
            bytes_accessed=2 * hidden * (hidden + 2 * width + tokens),
            transcendentals=hidden * tokens,
        ),
    )(inputs, first_factor.reshape(width, hidden), second_factor.reshape(hidden, hidden), cotangent)
    return input_grad, first_grad.reshape(rows, 1, hidden)


def solution(mesh, z_hi=Z_HI):
    return jax.shard_map(
        functools.partial(body, mesh.shape["dp"], mesh.shape["tensor"], z_hi),
        mesh=mesh,
        in_specs=(
            P("dp", "tensor"),
            P(None, "tensor", None),
            P(None, "tensor", None),
            P("tensor", "dp"),
        ),
        out_specs=(P("dp", "tensor"), P("dp", "tensor", None)),
        check_vma=False,
    )
```

time: 647 us -> 76.2 us (0.12)
  waiting for transfers between devices: 588 us -> 0 us
  Pallas kernels: 0 us -> 68.7 us
  blocking collectives: 14.5 us -> 0 us
  between operations: 14.7 us -> 0.65 us
  starting transfers between devices: 11 us -> 0 us
  matrix products: 8.65 us -> 0 us
    unnamed x2 -> x0, waiting for transfers between devices: 577 us -> none
    pallas_call x0 -> x1, Pallas kernels: none -> 68.7 us  [body(): pl.pallas_call(functools.partial(kernel, (nx, nz, ny, chunks, groups), (t...]
    all_to_all x1 -> x0, blocking collectives: 14.5 us -> none  [body(): lax.all_to_all(mixed_grad.reshape(local, blocks, group, tokens_here), 'te...]
    all_to_all x1 -> x0, starting transfers between devices: 11 us -> none  [body(): lax.all_to_all(outgoing, 'tensor', split_axis=0, concat_axis=1, tiled=True)]
    all_to_all x1 -> x0, waiting for transfers between devices: 10.9 us -> none  [body(): lax.all_to_all(outgoing, 'tensor', split_axis=0, concat_axis=1, tiled=True)]
    dot_general x4 -> x0, matrix products: 8.65 us -> none  [the longest x1 3.96 us: body(): jnp.einsum('lnt,mln->lmt', pre_grad, second_factor, preferred_element_typ...]
  transfers between devices with their start and end apart: 2 -> 0, of which waited for: 2 -> 0; matrix products, arithmetic and copies ran while one was open for 1% -> 0% of each run, Pallas kernels for 0% -> 0%
where the time goes in v1:
time: 76.2 us; the launch traced here: 75.2 us
  Pallas kernels  68.7 us (90%)
  local copies, waits for them, and re-layouts  5.85 us (8%)
    pallas_call x1, Pallas kernels, body(): pl.pallas_call(functools.partial(kernel, (nx, nz, ny, chunks, groups), (t...  68.7 us
    unnamed x10, local copies, waits for them, and re-layouts  5.85 us

profile of v1, /device:TPU:1, one launch (start us, length us, event | category | flops | bytes accessed | tf_op | source)
XLA Modules:
  0.0 75.2 jit_solution(16132809188417403759)
XLA Ops:
  0.6 0.0 copy-start
  0.6 1.6 %copy-done = bf16[1024,1,1024]{2,0,1:T(8,128)(2,1)S(1)} copy-done((bf16[1024,1,1024]{2,0,1:T(8,128)(2,1)S(1)}, bf16[1024,1,1024]{2,0,1:T(8,128)(2,1)}, u32[]{:S(2)}) %copy-start) | copy-done | bytes 2097176
  2.2 0.0 copy-start.1
  2.2 1.0 %copy-done.1 = bf16[256,1,1024]{2,0,1:T(8,128)(2,1)S(1)} copy-done((bf16[256,1,1024]{2,0,1:T(8,128)(2,1)S(1)}, bf16[256,1,1024]{2,0,1:T(8,128)(2,1)}, u32[]{:S(2)}) %copy-start.1) | copy-done | bytes 524312
  3.3 0.0 copy-start.2
  3.3 1.0 %copy-done.2 = bf16[1024,256]{1,0:T(8,128)(2,1)S(1)} copy-done((bf16[1024,256]{1,0:T(8,128)(2,1)S(1)}, bf16[1024,256]{1,0:T(8,128)(2,1)}, u32[]{:S(2)}) %copy-start.2) | copy-done | bytes 524312
  4.3 0.0 copy-start.3
  4.3 0.9 %copy-done.3 = bf16[256,256]{1,0:T(8,128)(2,1)S(1)} copy-done((bf16[256,256]{1,0:T(8,128)(2,1)S(1)}, bf16[256,256]{1,0:T(8,128)(2,1)}, u32[]{:S(2)}) %copy-start.3) | copy-done | bytes 131096
  5.2 68.7 %shard_map.59 = (bf16[256,256]{1,0:T(8,128)(2,1)S(1)}, f32[4,1024]{1,0:T(4,128)S(1)}) custom-call(bf16[256,256]{1,0:T(8,128)(2,1)S(1)} %copy-done.3, bf16[256,1024]{1,0:T(8,128)(2,1)S(1)} %bitcast.5, bf16[1024,1024]{1,0:T(8,128)(2,1)S(1)} %bitcast.4, bf16[1024,256]{1,0:T(8,128)(2,1)S(1)} %copy-done.2), custom_call_target="tpu_custom_call" | custom-call | flops 1476395008 | bytes 3670016 | tf_op jit(solution)/shard_map/pallas_call | solution.py:351
  73.9 0.6 copy.6
  74.6 0.7 copy.8
Async XLA Ops:
  0.6 1.6 %copy-start = (bf16[1024,1,1024]{2,0,1:T(8,128)(2,1)S(1)}, bf16[1024,1,1024]{2,0,1:T(8,128)(2,1)}, u32[]{:S(2)}) copy-start(bf16[1024,1,1024]{2,0,1:T(8,128)(2,1)} %param.6) | copy-start | bytes 6291460
  2.2 1.0 %copy-start.1 = (bf16[256,1,1024]{2,0,1:T(8,128)(2,1)S(1)}, bf16[256,1,1024]{2,0,1:T(8,128)(2,1)}, u32[]{:S(2)}) copy-start(bf16[256,1,1024]{2,0,1:T(8,128)(2,1)} %param.5) | copy-start | bytes 1572868
  3.3 1.0 %copy-start.2 = (bf16[1024,256]{1,0:T(8,128)(2,1)S(1)}, bf16[1024,256]{1,0:T(8,128)(2,1)}, u32[]{:S(2)}) copy-start(bf16[1024,256]{1,0:T(8,128)(2,1)} %cot_hbm.1) | copy-start | bytes 1572868
  4.3 0.9 %copy-start.3 = (bf16[256,256]{1,0:T(8,128)(2,1)S(1)}, bf16[256,256]{1,0:T(8,128)(2,1)}, u32[]{:S(2)}) copy-start(bf16[256,256]{1,0:T(8,128)(2,1)} %x_hbm.1) | copy-start | bytes 393220

commit v2 on v1

--- a/solution.py
+++ b/solution.py
@@ -30,9 +30,9 @@
     ig_ref, fg_ref,
     x_ref, f_ref, s_ref, cot_ref, st_ref, xpt_ref, pg_ref,
     out_buf, mix_buf, grad_buf, ret_buf,
-    term_buf, core_land, x_send, x_land, z_send, z_land,
+    term_buf, core_land, xz_send_1, zx_send_1, xz_land_1, zx_land_1, xz_send_2, zx_send_2, xz_land_2, zx_land_2,
     load_sem, out_ssem, out_rsem, ret_ssem, ret_rsem,
-    core_ssem, core_rsem, x_ssem, x_rsem, z_ssem, z_rsem,
+    core_ssem, core_rsem, xz_ssem_1, zx_ssem_1, xz_rsem_1, zx_rsem_1, xz_ssem_2, zx_ssem_2, xz_rsem_2, zx_rsem_2,
 ):
     nx, nz, ny, chunks, groups = dims
     per = ny // groups
@@ -157,12 +157,17 @@
     row = lax.broadcasted_iota(jnp.int32, (width, width), 0)
     col = lax.broadcasted_iota(jnp.int32, (width, width), 1)
     half = width // CORES
-    r_in = row & (rows - 1)
-    z_in = (row & (rows * nz - 1)) - r_in
-    x_in = (row & (half - 1)) - z_in - r_in
-    c_in = jnp.where(row >= half, rows, 0)
-    pick = jnp.where(x_in * CORES + z_in * CORES + c_in + r_in == col, 1.0, 0.0).astype(BF16)
-    xpt_ref[...] = dot(pick, x_ref[...], ((1,), (1,))).astype(BF16)
+    from_core = jnp.where(row >= half, rows, 0)
+    r_at = row & (rows - 1)
+    unit = row >> (rows.bit_length() - 1)
+    for kind in range(2):
+        if kind:
+            z_at, x_at = (unit >> (nx.bit_length() - 1)) & (nz - 1), unit & (nx - 1)
+        else:
+            x_at, z_at = (unit >> (nz.bit_length() - 1)) & (nx - 1), unit & (nz - 1)
+        taken = (x_at * nz + z_at) * (CORES * rows) + from_core + r_at
+        pick = jnp.where(taken == col, 1.0, 0.0).astype(BF16)
+        xpt_ref[kind] = dot(pick, x_ref[...], ((1,), (1,))).astype(BF16)
     loads[2].wait()
     tile = min(256, hidden)
     for i in range(hidden // tile):
@@ -206,29 +211,48 @@
         send_ret(c, ny - 1, 1)
         ret_buf[c, tp] = grad_buf[c, tp]
 
+    lane = per // 2
+    place, count = (x, z), (nx, nz)
+    send_1, land_1, ssem_1, rsem_1 = (
+        (xz_send_1, zx_send_1), (xz_land_1, zx_land_1), (xz_ssem_1, zx_ssem_1), (xz_rsem_1, zx_rsem_1)
+    )
+    send_2, land_2, ssem_2, rsem_2 = (
+        (xz_send_2, zx_send_2), (xz_land_2, zx_land_2), (xz_ssem_2, zx_ssem_2), (xz_rsem_2, zx_rsem_2)
+    )
+
     def to_core(g):
         return pltpu.make_async_remote_copy(
             term_buf.at[g, 1 - core], core_land.at[g], core_ssem.at[g], core_rsem.at[g],
             device_id=(sibling, tp), device_id_type=MESH,
         )
 
-    def to_x(g, i):
-        other = lax.rem(x + i, nx)
+    def to_first(kind, g, i):
+        other = lax.rem(place[kind] + i, count[kind])
+        to = dp_of(x, other, core) if kind else dp_of(other, z, core)
         return pltpu.make_async_remote_copy(
-            x_send.at[g, other], x_land.at[g, i], x_ssem.at[g, i], x_rsem.at[g, i],
-            device_id=(dp_of(other, z, core), tp), device_id_type=MESH,
+            send_1[kind].at[g, other], land_1[kind].at[g, i], ssem_1[kind].at[g, i], rsem_1[kind].at[g, i],
+            device_id=(to, tp), device_id_type=MESH,
         )
 
-    def to_z(g, i):
-        other = lax.rem(z + i, nz)
+    def to_second(kind, g, i):
+        other = lax.rem(place[1 - kind] + i, count[1 - kind])
+        to = dp_of(other, z, core) if kind else dp_of(x, other, core)
         return pltpu.make_async_remote_copy(
-            z_send.at[g, other], z_land.at[g, i], z_ssem.at[g, i], z_rsem.at[g, i],
-            device_id=(dp_of(x, other, core), tp), device_id_type=MESH,
+            send_2[kind].at[g, other], land_2[kind].at[g, i], ssem_2[kind].at[g, i], rsem_2[kind].at[g, i],
+            device_id=(to, tp), device_id_type=MESH,
         )
+
+    def each(n, act):
+        def go(i, _):
+            act(i)
+            return 0
+
+        lax.fori_loop(1, n, go, 0)
 
     def stage_a(g):
         for p in range(per):
             s = g * per + p
+            kind = p // lane
             for c in range(chunks):
                 for dz in range(Z_LO):
                     if s < ny - 1 or dz:
@@ -237,7 +261,7 @@
             term = jnp.zeros((width, pair), F32)
             for c in range(chunks):
                 term += dot(
-                    xpt_ref[:, c * tc : (c + 1) * tc], ret_buf[c, at].reshape(pair, tc), ((1,), (1,))
+                    xpt_ref[kind, :, c * tc : (c + 1) * tc], ret_buf[c, at].reshape(pair, tc), ((1,), (1,))
                 )
             term_buf[g, 0, p] = term[:half]
             term_buf[g, 1, p] = term[half:]
@@ -245,66 +269,55 @@
 
     def stage_b(g):
         to_core(g).wait_recv()
-        for p in range(per):
-            total = term_buf[g, core, p] + core_land[g, p]
-            core_land[g, p] = total
-            x_send[g, :, p] = total.astype(BF16).reshape(nx, half // nx, pair)
-
-        def go(i, _):
-            to_x(g, i).start()
-            return 0
-
-        lax.fori_loop(1, nx, go, 0)
+        for kind in range(2):
+            n = count[kind]
+            for q in range(lane):
+                p = kind * lane + q
+                total = term_buf[g, core, p] + core_land[g, p]
+                core_land[g, p] = total
+                send_1[kind][g, :, q] = total.astype(BF16).reshape(n, half // n, pair)
+            each(n, lambda i: to_first(kind, g, i).start())
 
     def stage_c(g):
-        part = half // nx
-
-        def arrive(i, _):
-            to_x(g, i).wait_recv()
-            return 0
-
-        lax.fori_loop(1, nx, arrive, 0)
-        total = core_land[g, :, pl.ds(pl.multiple_of(x * part, part), part)]
-        for i in range(1, nx):
-            total += x_land[g, i].astype(F32)
-        for i in range(nz):
-            z_send[g, i] = total[:, i * rows : (i + 1) * rows]
-
-        def go(i, _):
-            to_z(g, i).start()
-            return 0
-
-        lax.fori_loop(1, nz, go, 0)
+        for kind in range(2):
+            n = count[kind]
+            part = half // n
+            each(n, lambda i: to_first(kind, g, i).wait_recv())
+            mine = pl.ds(pl.multiple_of(place[kind] * part, part), part)
+            total = core_land[g, kind * lane : (kind + 1) * lane, mine]
+            for i in range(1, n):
+                total += land_1[kind][g, i].astype(F32)
+            for i in range(count[1 - kind]):
+                send_2[kind][g, i] = total[:, i * rows : (i + 1) * rows]
+            each(count[1 - kind], lambda i: to_second(kind, g, i).start())
 
     def stage_d(g):
-        def arrive(i, _):
-            to_z(g, i).wait_recv()
-            return 0
-
-        lax.fori_loop(1, nz, arrive, 0)
-        total = z_send[g, z]
-        for i in range(1, nz):
-            total += z_land[g, i]
-        for p in range(per):
-            at = pl.ds(pl.multiple_of(y_from(g * per + p) * pair, pair), pair)
-            fg_ref[:, at] = total[p] * scale
+        for kind in range(2):
+            n = count[1 - kind]
+            each(n, lambda i: to_second(kind, g, i).wait_recv())
+            total = send_2[kind][g, place[1 - kind]]
+            for i in range(1, n):
+                total += land_2[kind][g, i]
+            for q in range(lane):
+                s = g * per + kind * lane + q
+                at = pl.ds(pl.multiple_of(y_from(s) * pair, pair), pair)
+                fg_ref[:, at] = total[q] * scale
 
     def input_grad():
         for c in range(chunks):
             made = dot(f_ref[...], ret_buf[c].reshape(hidden, tc))
             ig_ref[c * tc : (c + 1) * tc, :] = made.T.astype(BF16)
 
-    for i in range(groups + 3):
-        if i < groups:
-            stage_a(i)
-        if i == groups - 1:
-            input_grad()
-        if 0 <= i - 1 < groups:
-            stage_b(i - 1)
-        if 0 <= i - 2 < groups:
-            stage_c(i - 2)
-        if 0 <= i - 3 < groups:
-            stage_d(i - 3)
+    for g in range(groups):
+        stage_a(g)
+        if g:
+            stage_b(g - 1)
+    stage_b(groups - 1)
+    input_grad()
+    for g in range(groups):
+        stage_c(g)
+    for g in range(groups):
+        stage_d(g)
 
     for c in range(chunks):
 
@@ -319,18 +332,9 @@
         exchange(grad_buf, ret_buf, ret_ssem, ret_rsem, c, ny - 1, 1).wait_send()
     for g in range(groups):
         to_core(g).wait_send()
-
-        def gone_x(i, _):
-            to_x(g, i).wait_send()
-            return 0
-
-        lax.fori_loop(1, nx, gone_x, 0)
-
-        def gone_z(i, _):
-            to_z(g, i).wait_send()
-            return 0
-
-        lax.fori_loop(1, nz, gone_z, 0)
+        for kind in range(2):
+            each(count[kind], lambda i: to_first(kind, g, i).wait_send())
+            each(count[1 - kind], lambda i: to_second(kind, g, i).wait_send())
 
 
 def body(n_dp, n_tensor, z_hi, inputs, first_factor, second_factor, cotangent):
@@ -338,14 +342,15 @@
     hidden = first_factor.shape[2]
     nz, ny = z_hi, n_tensor // Z_LO
     nx = n_dp // (nz * CORES)
-    chunks, groups = 2, min(4, ny)
+    chunks, groups = 2, min(2, ny // 2)
     per = ny // groups
     tc = tokens // chunks
     span = hidden // n_tensor
     pair = span * Z_LO
     half = width // CORES
-    part = half // nx
-    rows = part // nz
+    rows = half // (nx * nz)
+    firsts = [pltpu.VMEM((groups, n, per // 2, half // n, pair), BF16) for n in (nx, nz)]
+    seconds = [pltpu.VMEM((groups, n, per // 2, rows, pair), F32) for n in (nz, nx)]
     dma = pltpu.SemaphoreType.DMA
     flow = pltpu.VMEM((chunks, n_tensor, span, tc), BF16)
     input_grad, first_grad = pl.pallas_call(
@@ -362,24 +367,21 @@
             pltpu.VMEM((hidden, hidden), BF16),
             pltpu.VMEM((hidden, tokens), BF16),
             pltpu.VMEM((hidden, hidden), BF16),
-            pltpu.VMEM((width, tokens), BF16),
+            pltpu.VMEM((2, width, tokens), BF16),
             pltpu.VMEM((hidden, tc), BF16),
             flow, flow, flow, flow,
             pltpu.VMEM((groups, CORES, per, half, pair), F32),
             pltpu.VMEM((groups, per, half, pair), F32),
-            pltpu.VMEM((groups, nx, per, part, pair), BF16),
-            pltpu.VMEM((groups, nx, per, part, pair), BF16),
-            pltpu.VMEM((groups, nz, per, rows, pair), F32),
-            pltpu.VMEM((groups, nz, per, rows, pair), F32),
+            *firsts, *firsts, *seconds, *seconds,
             dma((4,)),
             dma((chunks, n_tensor)), dma((chunks, n_tensor)),
             dma((chunks, n_tensor)), dma((chunks, n_tensor)),
             dma((groups,)), dma((groups,)),
-            dma((groups, nx)), dma((groups, nx)),
-            dma((groups, nz)), dma((groups, nz)),
+            dma((groups, nx)), dma((groups, nz)), dma((groups, nx)), dma((groups, nz)),
+            dma((groups, nz)), dma((groups, nx)), dma((groups, nz)), dma((groups, nx)),
         ],
         compiler_params=pltpu.CompilerParams(
-            collective_id=0, has_side_effects=True, vmem_limit_bytes=40 * 2**20
+            collective_id=0, has_side_effects=True, vmem_limit_bytes=60 * 2**20
         ),
         cost_estimate=pl.CostEstimate(
             flops=2 * tokens * hidden * (2 * hidden + 3 * width),

time: 76.2 us -> 67.6 us (0.89); the launches traced: 75.2 us -> 67.4 us
  Pallas kernels: 68.7 us -> 63.9 us
  local copies, waits for them, and re-layouts: 5.85 us -> 2.91 us
    pallas_call x1, Pallas kernels: 68.7 us -> 63.9 us  [body(): pl.pallas_call(functools.partial(kernel, (nx, nz, ny, chunks, groups), (t...]
    unnamed x10 -> x2, local copies, waits for them, and re-layouts: 5.85 us -> 2.91 us
where the time goes in v2:
time: 67.6 us; the launch traced here: 67.4 us
  Pallas kernels  63.9 us (95%)
  local copies, waits for them, and re-layouts  2.91 us (4%)
    pallas_call x1, Pallas kernels, body(): pl.pallas_call(functools.partial(kernel, (nx, nz, ny, chunks, groups), (t...  63.9 us
    unnamed x2, local copies, waits for them, and re-layouts  2.91 us

profile of v2, /device:TPU:1, one launch (start us, length us, event | category | flops | bytes accessed | tf_op | source)
XLA Modules:
  0.0 67.4 jit_solution(9902387683748845254)
XLA Ops:
  0.6 63.9 %shard_map.59 = (bf16[256,256]{1,0:T(8,128)(2,1)}, f32[4,1024]{1,0:T(4,128)}) custom-call(bf16[256,256]{1,0:T(8,128)(2,1)} %x_hbm.1, bf16[256,1024]{1,0:T(8,128)(2,1)} %bitcast.5, bf16[1024,1024]{1,0:T(8,128)(2,1)} %bitcast.4, bf16[1024,256]{1,0:T(8,128)(2,1)} %cot_hbm.1), custom_call_target="tpu_custom_call" | custom-call | flops 1476395008 | bytes 3670016 | tf_op jit(solution)/shard_map/pallas_call | solution.py:356
  64.5 1.3 %copy.6 = f32[4,1,1024]{2,1,0:T(1,128)} copy(f32[4,1,1024]{2,0,1:T(4,128)} %bitcast.3) | data formatting | bytes 32768
  65.9 1.6 %copy.8 = bf16[256,256]{1,0:T(8,128)(2,1)} copy(bf16[256,256]{1,0:T(8,128)(2,1)} %get-tuple-element.10) | data formatting | bytes 262144

commit v3 on v2

--- a/solution.py
+++ b/solution.py
@@ -54,7 +54,9 @@
         return (xi * nz + zi) * CORES + ci
 
     def shift(s):
-        return ny // 2 + (1 - 2 * lax.rem(s, 2)) * ((s + 1) // 2)
+        k = ny // 2 - 1 - s // 2
+        odd = lax.rem(s, 2)
+        return k + odd * (ny - 2 * k) + (s // (ny - 2)) * (1 - odd) * (ny // 2)
 
     def y_to(s):
         return lax.rem(y + shift(s), ny)
@@ -96,27 +98,20 @@
     sibling = dp_of(x, z, 1 - core)
     pl.semaphore_signal(barrier, inc=1, device_id=(sibling, tp), device_id_type=MESH)
 
+    def taken(buf, index, sem):
+        return pltpu.make_async_copy(buf.at[index], buf.at[index], sem)
+
     def exchange(src, dst, ssem, rsem, c, s, dz):
         to = y_to(s) * Z_LO + lax.rem(zl + dz, Z_LO)
-        i = s * Z_LO + dz
         return pltpu.make_async_remote_copy(
-            src.at[c, to], dst.at[c, tp], ssem.at[c, i], rsem.at[c, i],
-            device_id=(dp, to), device_id_type=MESH,
+            src.at[c, to], dst.at[c, tp], ssem, rsem, device_id=(dp, to), device_id_type=MESH
         )
 
-    def landed(dst, ssem, rsem, c, s, dz):
-        here = y_from(s) * Z_LO + lax.rem(zl + dz, Z_LO)
-        i = s * Z_LO + dz
-        pltpu.make_async_remote_copy(
-            dst.at[c, here], dst.at[c, here], ssem.at[c, i], rsem.at[c, i],
-            device_id=(dp, tp), device_id_type=MESH,
-        ).wait_recv()
-
     def send_out(c, s, dz):
-        exchange(out_buf, mix_buf, out_ssem, out_rsem, c, s, dz).start()
-
-    def send_ret(c, s, dz):
-        exchange(grad_buf, ret_buf, ret_ssem, ret_rsem, c, s, dz).start()
+        exchange(out_buf, mix_buf, out_ssem.at[c], out_rsem.at[c], c, s, dz).start()
+
+    def send_ret(c, g, s, dz):
+        exchange(grad_buf, ret_buf, ret_ssem.at[c], ret_rsem.at[c, g], c, s, dz).start()
 
     loads[0].wait()
     loads[1].wait()
@@ -128,31 +123,37 @@
         for c in range(chunks):
             out_buf[c, pl.ds(to * Z_LO, Z_LO)] = made[:, c * tc : (c + 1) * tc].reshape(Z_LO, span, tc)
 
+    def send_all(send, c, start, stop):
+        def far(s, _):
+            send(c, s, 1)
+            return 0
+
+        def near(s, _):
+            send(c, s, 0)
+            return 0
+
+        lax.fori_loop(start, stop, far, 0)
+        lax.fori_loop(start, min(stop, ny - 1), near, 0)
+
     first(0)
     pl.semaphore_wait(barrier, (nt - 1) + (nx - 1) + (nz - 1) + 1)
-    for dz in range(Z_LO):
-        send_out(0, 0, dz)
+    send_out(0, 0, 1)
 
     def first_step(s, _):
         first(s)
-        for dz in range(Z_LO):
-            send_out(0, s, dz)
+        send_out(0, s, 1)
         return 0
 
-    lax.fori_loop(1, ny - 1, first_step, 0)
-    first(ny - 1)
-    send_out(0, ny - 1, 1)
+    def first_near(s, _):
+        send_out(0, s, 0)
+        return 0
+
+    lax.fori_loop(1, ny, first_step, 0)
+    lax.fori_loop(0, ny - 1, first_near, 0)
+    for c in range(1, chunks):
+        send_all(send_out, c, 0, ny)
     for c in range(chunks):
         mix_buf[c, tp] = out_buf[c, tp]
-    for c in range(1, chunks):
-
-        def rest(s, _):
-            for dz in range(Z_LO):
-                send_out(c, s, dz)
-            return 0
-
-        lax.fori_loop(0, ny - 1, rest, 0)
-        send_out(c, ny - 1, 1)
 
     row = lax.broadcasted_iota(jnp.int32, (width, width), 0)
     col = lax.broadcasted_iota(jnp.int32, (width, width), 1)
@@ -165,8 +166,8 @@
             z_at, x_at = (unit >> (nx.bit_length() - 1)) & (nz - 1), unit & (nx - 1)
         else:
             x_at, z_at = (unit >> (nz.bit_length() - 1)) & (nx - 1), unit & (nz - 1)
-        taken = (x_at * nz + z_at) * (CORES * rows) + from_core + r_at
-        pick = jnp.where(taken == col, 1.0, 0.0).astype(BF16)
+        source = (x_at * nz + z_at) * (CORES * rows) + from_core + r_at
+        pick = jnp.where(source == col, 1.0, 0.0).astype(BF16)
         xpt_ref[kind] = dot(pick, x_ref[...], ((1,), (1,))).astype(BF16)
     loads[2].wait()
     tile = min(256, hidden)
@@ -176,13 +177,7 @@
 
     for c in range(chunks):
 
-        def arrive(s, _):
-            for dz in range(Z_LO):
-                landed(mix_buf, out_ssem, out_rsem, c, s, dz)
-            return 0
-
-        lax.fori_loop(0, ny - 1, arrive, 0)
-        landed(mix_buf, out_ssem, out_rsem, c, ny - 1, 1)
+        taken(mix_buf, (c, pl.ds(0, nt - 1)), out_rsem.at[c]).wait()
 
         def forward(i, _):
             at = pl.ds(pl.multiple_of(i * tile, tile), tile)
@@ -194,21 +189,29 @@
 
         lax.fori_loop(0, hidden // tile, forward, 0)
 
-        def back(s):
-            to = y_to(s)
-            block = s_ref[pl.ds(pl.multiple_of(to * pair, pair), pair), :]
-            made = dot(block, pg_ref[...]).astype(BF16)
-            grad_buf[c, pl.ds(to * Z_LO, Z_LO)] = made.reshape(Z_LO, span, tc)
-
-        def back_step(s, _):
-            back(s)
-            for dz in range(Z_LO):
-                send_ret(c, s, dz)
-            return 0
-
-        lax.fori_loop(0, ny - 1, back_step, 0)
-        back(ny - 1)
-        send_ret(c, ny - 1, 1)
+        def back(i):
+            ends = [y_to(2 * i + j) for j in range(2)]
+            block = jnp.concatenate(
+                [s_ref[pl.ds(pl.multiple_of(to * pair, pair), pair), :] for to in ends], axis=0
+            )
+            made = dot(block, pg_ref[...]).astype(BF16).reshape(2, Z_LO, span, tc)
+            for j in range(2):
+                grad_buf[c, pl.ds(ends[j] * Z_LO, Z_LO)] = made[j]
+
+        for g in range(groups):
+
+            def back_step(i, _):
+                back(i)
+                for j in range(2):
+                    send_ret(c, g, 2 * i + j, 1)
+                return 0
+
+            def back_near(s, _):
+                send_ret(c, g, s, 0)
+                return 0
+
+            lax.fori_loop(g * per // 2, (g + 1) * per // 2, back_step, 0)
+            lax.fori_loop(g * per, min((g + 1) * per, ny - 1), back_near, 0)
         ret_buf[c, tp] = grad_buf[c, tp]
 
     lane = per // 2
@@ -230,7 +233,7 @@
         other = lax.rem(place[kind] + i, count[kind])
         to = dp_of(x, other, core) if kind else dp_of(other, z, core)
         return pltpu.make_async_remote_copy(
-            send_1[kind].at[g, other], land_1[kind].at[g, i], ssem_1[kind].at[g, i], rsem_1[kind].at[g, i],
+            send_1[kind].at[g, other], land_1[kind].at[g, i], ssem_1[kind].at[g], rsem_1[kind].at[g],
             device_id=(to, tp), device_id_type=MESH,
         )
 
@@ -238,7 +241,7 @@
         other = lax.rem(place[1 - kind] + i, count[1 - kind])
         to = dp_of(other, z, core) if kind else dp_of(x, other, core)
         return pltpu.make_async_remote_copy(
-            send_2[kind].at[g, other], land_2[kind].at[g, i], ssem_2[kind].at[g, i], rsem_2[kind].at[g, i],
+            send_2[kind].at[g, other], land_2[kind].at[g, i], ssem_2[kind].at[g], rsem_2[kind].at[g],
             device_id=(to, tp), device_id_type=MESH,
         )
 
@@ -250,13 +253,12 @@
         lax.fori_loop(1, n, go, 0)
 
     def stage_a(g):
+        came = per * Z_LO - (g == groups - 1)
+        for c in range(chunks):
+            taken(ret_buf, (c, pl.ds(0, came)), ret_rsem.at[c, g]).wait()
         for p in range(per):
             s = g * per + p
             kind = p // lane
-            for c in range(chunks):
-                for dz in range(Z_LO):
-                    if s < ny - 1 or dz:
-                        landed(ret_buf, ret_ssem, ret_rsem, c, s, dz)
             at = pl.ds(y_from(s) * Z_LO, Z_LO)
             term = jnp.zeros((width, pair), F32)
             for c in range(chunks):
@@ -282,7 +284,7 @@
         for kind in range(2):
             n = count[kind]
             part = half // n
-            each(n, lambda i: to_first(kind, g, i).wait_recv())
+            taken(land_1[kind], (g, pl.ds(1, n - 1)), rsem_1[kind].at[g]).wait()
             mine = pl.ds(pl.multiple_of(place[kind] * part, part), part)
             total = core_land[g, kind * lane : (kind + 1) * lane, mine]
             for i in range(1, n):
@@ -294,7 +296,7 @@
     def stage_d(g):
         for kind in range(2):
             n = count[1 - kind]
-            each(n, lambda i: to_second(kind, g, i).wait_recv())
+            taken(land_2[kind], (g, pl.ds(1, n - 1)), rsem_2[kind].at[g]).wait()
             total = send_2[kind][g, place[1 - kind]]
             for i in range(1, n):
                 total += land_2[kind][g, i]
@@ -314,27 +316,21 @@
             stage_b(g - 1)
     stage_b(groups - 1)
     input_grad()
+    for c in range(chunks):
+        taken(out_buf, (c, pl.ds(0, nt - 1)), out_ssem.at[c]).wait()
+        taken(grad_buf, (c, pl.ds(0, nt - 1)), ret_ssem.at[c]).wait()
+    for g in range(groups):
+        to_core(g).wait_send()
     for g in range(groups):
         stage_c(g)
     for g in range(groups):
+        for kind in range(2):
+            taken(send_1[kind], (g, pl.ds(1, count[kind] - 1)), ssem_1[kind].at[g]).wait()
+    for g in range(groups):
         stage_d(g)
-
-    for c in range(chunks):
-
-        def gone(s, _):
-            for dz in range(Z_LO):
-                exchange(out_buf, mix_buf, out_ssem, out_rsem, c, s, dz).wait_send()
-                exchange(grad_buf, ret_buf, ret_ssem, ret_rsem, c, s, dz).wait_send()
-            return 0
-
-        lax.fori_loop(0, ny - 1, gone, 0)
-        exchange(out_buf, mix_buf, out_ssem, out_rsem, c, ny - 1, 1).wait_send()
-        exchange(grad_buf, ret_buf, ret_ssem, ret_rsem, c, ny - 1, 1).wait_send()
-    for g in range(groups):
-        to_core(g).wait_send()
+    for g in range(groups):
         for kind in range(2):
-            each(count[kind], lambda i: to_first(kind, g, i).wait_send())
-            each(count[1 - kind], lambda i: to_second(kind, g, i).wait_send())
+            taken(send_2[kind], (g, pl.ds(1, count[1 - kind] - 1)), ssem_2[kind].at[g]).wait()
 
 
 def body(n_dp, n_tensor, z_hi, inputs, first_factor, second_factor, cotangent):
@@ -342,7 +338,7 @@
     hidden = first_factor.shape[2]
     nz, ny = z_hi, n_tensor // Z_LO
     nx = n_dp // (nz * CORES)
-    chunks, groups = 2, min(2, ny // 2)
+    chunks, groups = 2, min(4, ny // 2)
     per = ny // groups
     tc = tokens // chunks
     span = hidden // n_tensor
@@ -374,11 +370,8 @@
             pltpu.VMEM((groups, per, half, pair), F32),
             *firsts, *firsts, *seconds, *seconds,
             dma((4,)),
-            dma((chunks, n_tensor)), dma((chunks, n_tensor)),
-            dma((chunks, n_tensor)), dma((chunks, n_tensor)),
-            dma((groups,)), dma((groups,)),
-            dma((groups, nx)), dma((groups, nz)), dma((groups, nx)), dma((groups, nz)),
-            dma((groups, nz)), dma((groups, nx)), dma((groups, nz)), dma((groups, nx)),
+            dma((chunks,)), dma((chunks,)), dma((chunks,)), dma((chunks, groups)),
+            *[dma((groups,))] * 10,
         ],
         compiler_params=pltpu.CompilerParams(
             collective_id=0, has_side_effects=True, vmem_limit_bytes=60 * 2**20

time: 67.6 us -> 64.1 us (0.948)
  Pallas kernels: 63.9 us -> 60.4 us
    pallas_call x1, Pallas kernels: 63.9 us -> 60.4 us  [body(): pl.pallas_call(functools.partial(kernel, (nx, nz, ny, chunks, groups), (t...]
where the time goes in v3:
time: 64.1 us; the launch traced here: 63.9 us
  Pallas kernels  60.4 us (94%)
  local copies, waits for them, and re-layouts  2.91 us (5%)
    pallas_call x1, Pallas kernels, body(): pl.pallas_call(functools.partial(kernel, (nx, nz, ny, chunks, groups), (t...  60.4 us
    unnamed x2, local copies, waits for them, and re-layouts  2.91 us

profile of v3, /device:TPU:1, one launch (start us, length us, event | category | flops | bytes accessed | tf_op | source)
XLA Modules:
  0.0 63.9 jit_solution(160893328620064901)
XLA Ops:
  0.6 60.4 %shard_map.59 = (bf16[256,256]{1,0:T(8,128)(2,1)}, f32[4,1024]{1,0:T(4,128)}) custom-call(bf16[256,256]{1,0:T(8,128)(2,1)} %x_hbm.1, bf16[256,1024]{1,0:T(8,128)(2,1)} %bitcast.5, bf16[1024,1024]{1,0:T(8,128)(2,1)} %bitcast.4, bf16[1024,256]{1,0:T(8,128)(2,1)} %cot_hbm.1), custom_call_target="tpu_custom_call" | custom-call | flops 1476395008 | bytes 3670016 | tf_op jit(solution)/shard_map/pallas_call | solution.py:352
  61.0 1.3 %copy.6 = f32[4,1,1024]{2,1,0:T(1,128)} copy(f32[4,1,1024]{2,0,1:T(4,128)} %bitcast.3) | data formatting | bytes 32768
  62.3 1.6 %copy.8 = bf16[256,256]{1,0:T(8,128)(2,1)} copy(bf16[256,256]{1,0:T(8,128)(2,1)} %get-tuple-element.10) | data formatting | bytes 262144

commit v4 on v3

--- a/solution.py
+++ b/solution.py
@@ -374,7 +374,7 @@
             *[dma((groups,))] * 10,
         ],
         compiler_params=pltpu.CompilerParams(
-            collective_id=0, has_side_effects=True, vmem_limit_bytes=60 * 2**20
+            collective_id=0, has_side_effects=True, vmem_limit_bytes=55040 * 2**10
         ),
         cost_estimate=pl.CostEstimate(
             flops=2 * tokens * hidden * (2 * hidden + 3 * width),

time: 64.1 us -> 61.8 us (0.964)
  local copies, waits for them, and re-layouts: 2.91 us -> 1.28 us
  Pallas kernels: 60.4 us -> 59.7 us
    unnamed x2, local copies, waits for them, and re-layouts: 2.91 us -> 1.28 us
    pallas_call x1, Pallas kernels: 60.4 us -> 59.7 us  [body(): pl.pallas_call(functools.partial(kernel, (nx, nz, ny, chunks, groups), (t...]
where the time goes in v4:
time: 61.8 us; the launch traced here: 61.6 us
  Pallas kernels  59.7 us (97%)
  local copies, waits for them, and re-layouts  1.28 us (2%)
  between operations  0.64 us (1%)
    pallas_call x1, Pallas kernels, body(): pl.pallas_call(functools.partial(kernel, (nx, nz, ny, chunks, groups), (t...  59.7 us
    unnamed x2, local copies, waits for them, and re-layouts  1.28 us

profile of v4, /device:TPU:1, one launch (start us, length us, event | category | flops | bytes accessed | tf_op | source)
XLA Modules:
  0.0 61.6 jit_solution(10379425606885159245)
XLA Ops:
  0.6 59.7 %shard_map.59 = (bf16[256,256]{1,0:T(8,128)(2,1)S(1)}, f32[4,1024]{1,0:T(4,128)S(1)}) custom-call(bf16[256,256]{1,0:T(8,128)(2,1)} %x_hbm.1, bf16[256,1024]{1,0:T(8,128)(2,1)} %bitcast.5, bf16[1024,1024]{1,0:T(8,128)(2,1)} %bitcast.4, bf16[1024,256]{1,0:T(8,128)(2,1)} %cot_hbm.1), custom_call_target="tpu_custom_call" | custom-call | flops 1476395008 | bytes 3670016 | tf_op jit(solution)/shard_map/pallas_call | solution.py:352
  60.4 0.6 %copy.6 = f32[4,1,1024]{2,1,0:T(1,128)} copy(f32[4,1,1024]{2,0,1:T(4,128)S(1)} %bitcast.3) | data formatting | bytes 32768
  61.0 0.7 %copy.8 = bf16[256,256]{1,0:T(8,128)(2,1)} copy(bf16[256,256]{1,0:T(8,128)(2,1)S(1)} %get-tuple-element.10) | data formatting | bytes 262144

commit v5 on v4

--- a/solution.py
+++ b/solution.py
@@ -214,7 +214,6 @@
             lax.fori_loop(g * per, min((g + 1) * per, ny - 1), back_near, 0)
         ret_buf[c, tp] = grad_buf[c, tp]
 
-    lane = per // 2
     place, count = (x, z), (nx, nz)
     send_1, land_1, ssem_1, rsem_1 = (
         (xz_send_1, zx_send_1), (xz_land_1, zx_land_1), (xz_ssem_1, zx_ssem_1), (xz_rsem_1, zx_rsem_1)
@@ -233,7 +232,7 @@
         other = lax.rem(place[kind] + i, count[kind])
         to = dp_of(x, other, core) if kind else dp_of(other, z, core)
         return pltpu.make_async_remote_copy(
-            send_1[kind].at[g, other], land_1[kind].at[g, i], ssem_1[kind].at[g], rsem_1[kind].at[g],
+            send_1[kind].at[g // 2, other], land_1[kind].at[g // 2, i], ssem_1[kind].at[g // 2], rsem_1[kind].at[g // 2],
             device_id=(to, tp), device_id_type=MESH,
         )
 
@@ -241,69 +240,62 @@
         other = lax.rem(place[1 - kind] + i, count[1 - kind])
         to = dp_of(other, z, core) if kind else dp_of(x, other, core)
         return pltpu.make_async_remote_copy(
-            send_2[kind].at[g, other], land_2[kind].at[g, i], ssem_2[kind].at[g], rsem_2[kind].at[g],
+            send_2[kind].at[g // 2, other], land_2[kind].at[g // 2, i], ssem_2[kind].at[g // 2], rsem_2[kind].at[g // 2],
             device_id=(to, tp), device_id_type=MESH,
         )
 
     def each(n, act):
-        def go(i, _):
+        for i in range(1, n):
             act(i)
-            return 0
-
-        lax.fori_loop(1, n, go, 0)
 
     def stage_a(g):
         came = per * Z_LO - (g == groups - 1)
         for c in range(chunks):
             taken(ret_buf, (c, pl.ds(0, came)), ret_rsem.at[c, g]).wait()
         for p in range(per):
-            s = g * per + p
-            kind = p // lane
-            at = pl.ds(y_from(s) * Z_LO, Z_LO)
+            at = pl.ds(y_from(g * per + p) * Z_LO, Z_LO)
             term = jnp.zeros((width, pair), F32)
             for c in range(chunks):
                 term += dot(
-                    xpt_ref[kind, :, c * tc : (c + 1) * tc], ret_buf[c, at].reshape(pair, tc), ((1,), (1,))
+                    xpt_ref[g % 2, :, c * tc : (c + 1) * tc], ret_buf[c, at].reshape(pair, tc), ((1,), (1,))
                 )
             term_buf[g, 0, p] = term[:half]
             term_buf[g, 1, p] = term[half:]
         to_core(g).start()
 
     def stage_b(g):
+        kind, h = g % 2, g // 2
+        n = count[kind]
         to_core(g).wait_recv()
-        for kind in range(2):
-            n = count[kind]
-            for q in range(lane):
-                p = kind * lane + q
-                total = term_buf[g, core, p] + core_land[g, p]
-                core_land[g, p] = total
-                send_1[kind][g, :, q] = total.astype(BF16).reshape(n, half // n, pair)
-            each(n, lambda i: to_first(kind, g, i).start())
+        for p in range(per):
+            total = term_buf[g, core, p] + core_land[g, p]
+            core_land[g, p] = total
+            send_1[kind][h, :, p] = total.astype(BF16).reshape(n, half // n, pair)
+        each(n, lambda i: to_first(kind, g, i).start())
 
     def stage_c(g):
-        for kind in range(2):
-            n = count[kind]
-            part = half // n
-            taken(land_1[kind], (g, pl.ds(1, n - 1)), rsem_1[kind].at[g]).wait()
-            mine = pl.ds(pl.multiple_of(place[kind] * part, part), part)
-            total = core_land[g, kind * lane : (kind + 1) * lane, mine]
-            for i in range(1, n):
-                total += land_1[kind][g, i].astype(F32)
-            for i in range(count[1 - kind]):
-                send_2[kind][g, i] = total[:, i * rows : (i + 1) * rows]
-            each(count[1 - kind], lambda i: to_second(kind, g, i).start())
+        kind, h = g % 2, g // 2
+        n = count[kind]
+        part = half // n
+        taken(land_1[kind], (h, pl.ds(1, n - 1)), rsem_1[kind].at[h]).wait()
+        mine = pl.ds(pl.multiple_of(place[kind] * part, part), part)
+        total = core_land[g, :, mine]
+        for i in range(1, n):
+            total += land_1[kind][h, i].astype(F32)
+        for i in range(count[1 - kind]):
+            send_2[kind][h, i] = total[:, i * rows : (i + 1) * rows]
+        each(count[1 - kind], lambda i: to_second(kind, g, i).start())
 
     def stage_d(g):
-        for kind in range(2):
-            n = count[1 - kind]
-            taken(land_2[kind], (g, pl.ds(1, n - 1)), rsem_2[kind].at[g]).wait()
-            total = send_2[kind][g, place[1 - kind]]
-            for i in range(1, n):
-                total += land_2[kind][g, i]
-            for q in range(lane):
-                s = g * per + kind * lane + q
-                at = pl.ds(pl.multiple_of(y_from(s) * pair, pair), pair)
-                fg_ref[:, at] = total[q] * scale
+        kind, h = g % 2, g // 2
+        n = count[1 - kind]
+        taken(land_2[kind], (h, pl.ds(1, n - 1)), rsem_2[kind].at[h]).wait()
+        total = send_2[kind][h, place[1 - kind]]
+        for i in range(1, n):
+            total += land_2[kind][h, i]
+        for p in range(per):
+            at = pl.ds(pl.multiple_of(y_from(g * per + p) * pair, pair), pair)
+            fg_ref[:, at] = total[p] * scale
 
     def input_grad():
         for c in range(chunks):
@@ -324,13 +316,13 @@
     for g in range(groups):
         stage_c(g)
     for g in range(groups):
-        for kind in range(2):
-            taken(send_1[kind], (g, pl.ds(1, count[kind] - 1)), ssem_1[kind].at[g]).wait()
+        kind, h = g % 2, g // 2
+        taken(send_1[kind], (h, pl.ds(1, count[kind] - 1)), ssem_1[kind].at[h]).wait()
     for g in range(groups):
         stage_d(g)
     for g in range(groups):
-        for kind in range(2):
-            taken(send_2[kind], (g, pl.ds(1, count[1 - kind] - 1)), ssem_2[kind].at[g]).wait()
+        kind, h = g % 2, g // 2
+        taken(send_2[kind], (h, pl.ds(1, count[1 - kind] - 1)), ssem_2[kind].at[h]).wait()
 
 
 def body(n_dp, n_tensor, z_hi, inputs, first_factor, second_factor, cotangent):
@@ -345,8 +337,8 @@
     pair = span * Z_LO
     half = width // CORES
     rows = half // (nx * nz)
-    firsts = [pltpu.VMEM((groups, n, per // 2, half // n, pair), BF16) for n in (nx, nz)]
-    seconds = [pltpu.VMEM((groups, n, per // 2, rows, pair), F32) for n in (nz, nx)]
+    firsts = [pltpu.VMEM((groups // 2, n, per, half // n, pair), BF16) for n in (nx, nz)]
+    seconds = [pltpu.VMEM((groups // 2, n, per, rows, pair), F32) for n in (nz, nx)]
     dma = pltpu.SemaphoreType.DMA
     flow = pltpu.VMEM((chunks, n_tensor, span, tc), BF16)
     input_grad, first_grad = pl.pallas_call(
@@ -371,7 +363,7 @@
             *firsts, *firsts, *seconds, *seconds,
             dma((4,)),
             dma((chunks,)), dma((chunks,)), dma((chunks,)), dma((chunks, groups)),
-            *[dma((groups,))] * 10,
+            dma((groups,)), dma((groups,)), *[dma((groups // 2,))] * 8,
         ],
         compiler_params=pltpu.CompilerParams(
             collective_id=0, has_side_effects=True, vmem_limit_bytes=55040 * 2**10

time: 61.8 us -> 62.2 us (level)
  no operation moved by 1% of the time
where the time goes in v5:
time: 62.2 us; the launch traced here: 62.1 us
  Pallas kernels  60.2 us (97%)
  local copies, waits for them, and re-layouts  1.28 us (2%)
  between operations  0.64 us (1%)
    pallas_call x1, Pallas kernels, body(): pl.pallas_call(functools.partial(kernel, (nx, nz, ny, chunks, groups), (t...  60.2 us
    unnamed x2, local copies, waits for them, and re-layouts  1.28 us

profile of v5, /device:TPU:1, one launch (start us, length us, event | category | flops | bytes accessed | tf_op | source)
XLA Modules:
  0.0 62.1 jit_solution(17998098514475532974)
XLA Ops:
  0.6 60.2 %shard_map.59 = (bf16[256,256]{1,0:T(8,128)(2,1)S(1)}, f32[4,1024]{1,0:T(4,128)S(1)}) custom-call(bf16[256,256]{1,0:T(8,128)(2,1)} %x_hbm.1, bf16[256,1024]{1,0:T(8,128)(2,1)} %bitcast.5, bf16[1024,1024]{1,0:T(8,128)(2,1)} %bitcast.4, bf16[1024,256]{1,0:T(8,128)(2,1)} %cot_hbm.1), custom_call_target="tpu_custom_call" | custom-call | flops 1476395008 | bytes 3670016 | tf_op jit(solution)/shard_map/pallas_call | solution.py:344
  60.8 0.6 %copy.6 = f32[4,1,1024]{2,1,0:T(1,128)} copy(f32[4,1,1024]{2,0,1:T(4,128)S(1)} %bitcast.3) | data formatting | bytes 32768
  61.4 0.7 %copy.8 = bf16[256,256]{1,0:T(8,128)(2,1)} copy(bf16[256,256]{1,0:T(8,128)(2,1)S(1)} %get-tuple-element.10) | data formatting | bytes 262144
